TPU v7x, 32 devices: a whole 2x2x4 slice. The times are simulated.
32 devices in a mesh: alpha: 16 (over z, y, x), beta: 2 (over core).
Axes of the slice: x: 2, y: 2, z: 4, core: 2. Of those that a mesh axis runs over, the one named last changes fastest.
Arguments:
- coeffs: bfloat16 [128, 2, 256], P('alpha', None, 'beta'), may hold values from -6 to 6
- integrals: bfloat16 [484, 484], replicated, may hold values from -0.03125 to 0.03125
- beta_source: int32 [484, 256], P(None, 'beta'), may hold values from 0 to 255
- beta_sign: int32 [484, 256], P(None, 'beta'), may hold values from -1 to 1
- alpha_slots: int32 [16, 16, 4, 128], P('alpha'), may hold values from -1 to 483, as said below
Outputs:
- sigma: float32 [128, 2, 256], P('alpha', None, 'beta')
Inputs may be any that keep to these rules, and one draw needn't show every extreme that they name: alpha_slots[s, d, 0, q], [s, d, 1, q], [s, d, 2, q], [s, d, 3, q] are the source string within block s (below 8), the orbital pair (below 484), the target string within block d (below 8) and the sign (-1 or 1; 0 marks an empty slot, whose other entries mean nothing); in every draw some target block has all 128 slots live from every source block.
All inputs are finite; a program needn't handle non-finite values.
Results may differ from a plain program's by a relative error of at most 0.0029.
Values may be sent and summed in bfloat16 or wider, within the bound.
A program may use at most 64 MiB of HBM per device.

v0:
```python
import jax
import jax.numpy as jnp
from jax import lax
from jax.sharding import PartitionSpec as P


def local(coeffs, integrals, beta_source, beta_sign, alpha_slots):
    strings = coeffs.shape[0]
    beta_cols = coeffs.shape[2]
    pair_count = integrals.shape[0]
    all_cols = lax.all_gather(coeffs, "beta", axis=2, tiled=True)
    cols_mat = all_cols.reshape(strings * 2, all_cols.shape[2])
    taken = jnp.take(cols_mat, beta_source, axis=1)
    dvec = taken * beta_sign.astype(jnp.bfloat16)[None]
    evec_sum = jnp.einsum("kp,xpb->kxb", integrals, dvec, preferred_element_type=jnp.float32)
    flat_rows = evec_sum.astype(jnp.bfloat16).reshape(pair_count * strings, 2 * beta_cols)
    slot_table = alpha_slots[0]
    source_ids = slot_table[:, 0]
    pair_ids = slot_table[:, 1]
    target_ids = slot_table[:, 2]
    sign_vals = slot_table[:, 3]
    row_ids = pair_ids * strings + source_ids
    picked = jnp.take(flat_rows, row_ids.reshape(-1), axis=0).reshape(
        source_ids.shape + (2 * beta_cols,)
    )
    buffer = picked * sign_vals.astype(jnp.bfloat16)[:, :, None]
    string_ids = jnp.arange(strings, dtype=jnp.int32)
    moved_rows, moved_targets = (
        lax.all_to_all(buffer, "alpha", split_axis=0, concat_axis=0, tiled=True),
        lax.all_to_all(target_ids, "alpha", split_axis=0, concat_axis=0, tiled=True),
    )
    one_hot = (moved_targets[:, :, None] == string_ids).astype(jnp.bfloat16)
    sigma = jnp.einsum("dqa,dqx->ax", one_hot, moved_rows, preferred_element_type=jnp.float32)
    return sigma.reshape(strings, 2, beta_cols)


def solution(mesh):
    in_specs = (
        P("alpha", None, "beta"),
        P(),
        P(None, "beta"),
        P(None, "beta"),
        P("alpha", None, None, None),
    )
    out_specs = P("alpha", None, "beta")
    return jax.shard_map(local, mesh=mesh, in_specs=in_specs, out_specs=out_specs, check_vma=False)
```

profile of v0, /device:TPU:0, one launch (start us, length us, event | category | flops | bytes accessed | tf_op | source)
XLA Modules:
  0.0 197.8 jit_solution(8219390977062383857)
XLA Ops:
  0.0 0.0 copy-start
  0.0 0.8 copy.21
  0.8 0.6 fusion.14
  1.4 8.3 %all-to-all-start = ((s32[16,1,128]{2,1,0:T(1,128)}), s32[16,1,128]{2,1,0:T(1,128)S(1)}, u32[]{:S(2)}, u32[]{:S(2)}) async-start(s32[16,1,128]{2,1,0:T(1,128)} %bitcast.1), calls=%async_computation | async-start | bytes 16384 | tf_op jit(solution)/shard_map/all_to_all | solution.py:30
  9.7 1.0 fusion.10
  10.7 1.0 compare_and_fusion
  11.8 2.0 %all_gather.3 = bf16[8,2,256]{2,1,0:T(2,128)(2,1)S(1)} all-gather(bf16[8,2,128]{2,1,0:T(2,128)(2,1)} %param.5), channel_id=1, replica_groups=mesh['alpha'=16,'beta'=2] {'beta'}, dimensions={2}, use_global_device_ids=true | all-gather | bytes 12288 | tf_op jit(solution)/shard_map/all_gather | solution.py:11
  13.8 0.1 copy.16
  14.0 123.6 %gather_fusion = bf16[61952,16]{1,0:T(8,128)(2,1)} fusion(bf16[16,256]{0,1:T(8,128)(2,1)S(1)} %copy.16, s32[62464]{0:T(1024)S(1)} %pad_clamp_fusion), kind=kCustom, calls=%fused_computation | custom fusion | bytes 4212736 | tf_op jit(solution)/shard_map/jit(_take)/gather | solution.py:13
  137.6 0.0 copy-start.1
  137.6 12.2 %copy.17 = bf16[484,128,16]{1,0,2:T(8,128)(2,1)S(1)} copy(bf16[484,128,16]{2,1,0:T(8,128)(2,1)} %bitcast.32) | data formatting | bytes 3964928 | tf_op jit(solution)/shard_map/jit(_take)/gather | solution.py:13
  149.8 0.0 copy-done.1
  149.8 0.0 copy-done
  149.8 1.3 convert_bitcast_fusion
  151.1 1.6 copy.18
  152.7 2.6 %reshape.81 = bf16[3872,256]{1,0:T(8,128)(2,1)S(1)} reshape(bf16[484,16,128]{2,1,0:T(8,128)(2,1)} %copy.18) | data formatting | bytes 3964928 | tf_op jit(solution)/shard_map/reshape | solution.py:16
  155.4 7.5 %gather_fusion.1 = bf16[2048,256]{1,0:T(8,128)(2,1)S(1)} fusion(bf16[3872,256]{1,0:T(8,128)(2,1)S(1)} %reshape.81, s32[2048]{0:T(1024)S(1)} %broadcast_clamp_fusion), kind=kCustom, calls=%fused_computation.1 | custom fusion | bytes 2105344 | tf_op jit(solution)/shard_map/jit(_take)/gather | solution.py:23
  162.9 0.7 select_multiply_fusion
  163.6 0.0 all-to-all-done
  163.6 33.4 %all_to_all.11 = bf16[16,128,256]{2,1,0:T(8,128)(2,1)S(1)} all-to-all(bf16[16,128,256]{2,1,0:T(8,128)(2,1)S(1)} %select_multiply_fusion), channel_id=1, replica_groups=mesh['alpha'=16,'beta'=2] {'alpha'}, dimensions={0} | all-to-all | bytes 2097152 | tf_op jit(solution)/shard_map/all_to_all | solution.py:29
  196.9 0.2 convolution_bitcast_fusion
  197.2 0.6 copy.19
  (6 shorter events, 0.1 us)
Async XLA Ops:
  0.0 149.8 %copy-start = (bf16[484,484]{1,0:T(8,128)(2,1)S(1)}, bf16[484,484]{1,0:T(8,128)(2,1)}, u32[]{:S(2)}) copy-start(bf16[484,484]{1,0:T(8,128)(2,1)} %param.6) | copy-start | bytes 1405540
  1.4 162.2 %all-to-all-start = ((s32[16,1,128]{2,1,0:T(1,128)}), s32[16,1,128]{2,1,0:T(1,128)S(1)}, u32[]{:S(2)}, u32[]{:S(2)}) async-start(s32[16,1,128]{2,1,0:T(1,128)} %bitcast.1), calls=%async_computation | async-start | bytes 16384 | tf_op jit(solution)/shard_map/all_to_all | solution.py:30
  137.6 12.2 %copy-start.1 = (s32[484,128]{1,0:T(8,128)S(1)}, s32[484,128]{1,0:T(8,128)}, u32[]{:S(2)}) copy-start(s32[484,128]{1,0:T(8,128)} %param.8) | copy-start | bytes 743428
where the time goes:
time: 198 us
  local copies, waits for them, and re-layouts  149 us (75%)
  blocking collectives  35.4 us (18%)
  starting transfers between devices  8.31 us (4%)
  other arithmetic  3.39 us (2%)
    gather x2, local copies, waits for them, and re-layouts, local(): taken = jnp.take(cols_mat, beta_source, axis=1)  136 us
    all_to_all x1, blocking collectives, local(): lax.all_to_all(buffer, 'alpha', split_axis=0, concat_axis=0, tiled=True)  33.4 us
    all_to_all x1, starting transfers between devices, local(): lax.all_to_all(target_ids, 'alpha', split_axis=0, concat_axis=0, tiled=True)  8.31 us
    gather x1, local copies, waits for them, and re-layouts, local(): jnp.take(flat_rows, row_ids.reshape(-1), axis=0)  7.5 us
  transfers between devices with their start and end apart: 1, of which 0 were waited for; matrix products, arithmetic and copies ran while one was open for 77% of the time, Pallas kernels for 0%

commit v1 on v0

v1 whole, which is shorter than its diff:
```python
import functools

import jax
import jax.numpy as jnp
from jax import lax
from jax.experimental import pallas as pl
from jax.experimental.pallas import tpu as pltpu
from jax.sharding import PartitionSpec as P

MESH = pl.DeviceIdType.MESH
LANES = 128
F32 = jnp.float32
BF16 = jnp.bfloat16


def kernel(
    n_alpha, n_beta, cols, strings,
    coeffs_ref, ints_ref, source_ref, sign_ref, slots_ref, out_ref,
    table, wide, dvec, counts, blocks, sent, got,
    c_send, c_recv, b_send, b_recv,
):
    ia = lax.axis_index("alpha")
    ib = lax.axis_index("beta")
    pairs = ints_ref.shape[0]
    rows = 2 * strings

    barrier = pltpu.get_barrier_semaphore()
    for r in range(1, n_beta):
        pl.semaphore_signal(barrier, inc=1, device_id={"beta": lax.rem(ib + r, n_beta)}, device_id_type=MESH)
    for r in range(1, n_alpha):
        pl.semaphore_signal(barrier, inc=1, device_id={"alpha": lax.rem(ia + r, n_alpha)}, device_id_type=MESH)

    def count(j, carry):
        cap = slots_ref.shape[-1]
        pair_iota = lax.broadcasted_iota(jnp.int32, (pairs, cap), 0)
        code_iota = lax.broadcasted_iota(jnp.int32, (strings * strings, cap), 0)
        parts = []
        for half in range(2):
            entry = slots_ref[0, 2 * j + half]
            code = entry[0:1] * strings + entry[2:3]
            sign = entry[3:4].astype(F32)
            hot = jnp.where(pair_iota == entry[1:2], 1.0, 0.0).astype(BF16)
            coded = jnp.where(code_iota == code, sign, 0.0).astype(BF16)
            parts.append(lax.dot_general(coded, hot, (((1,), (1,)), ((), ())), preferred_element_type=F32))
        for a in range(strings):
            both = jnp.concatenate([part[a * strings:(a + 1) * strings] for part in parts], axis=0)
            counts[a, pl.ds(pl.multiple_of(j * rows, rows), rows), :] = both.astype(BF16)
        return carry

    first = n_alpha // 4
    lax.fori_loop(0, first, count, 0)
    pl.semaphore_wait(barrier, n_alpha + n_beta - 2)

    copies = []
    for r in range(1, n_beta):
        copy = pltpu.make_async_remote_copy(
            src_ref=coeffs_ref, dst_ref=table.at[r], send_sem=c_send.at[r], recv_sem=c_recv.at[r],
            device_id={"beta": lax.rem(ib + r, n_beta)}, device_id_type=MESH)
        copy.start()
        copies.append(copy)
    lax.fori_loop(first, n_alpha // 2, count, 0)
    for copy in copies:
        copy.wait()

    for r in range(n_beta):
        block = (coeffs_ref[...] if r == 0 else table[r]).astype(F32)
        for x in range(rows):
            wide[r, x] = jnp.broadcast_to(block[x:x + 1], (8, LANES))

    def take(src, sgn):
        lane = src & (cols - 1)
        step = lax.shift_right_logical(src, (cols - 1).bit_length())
        slot = (ib + n_beta - step) & (n_beta - 1)
        sgn = sgn.astype(F32)
        for x in range(rows):
            halves = []
            for h in (0, 8):
                index = lane[h:h + 8]
                which = slot[h:h + 8]
                value = jnp.take_along_axis(wide[0, x], index, axis=1)
                for r in range(1, n_beta):
                    value = jnp.where(which == r, jnp.take_along_axis(wide[r, x], index, axis=1), value)
                halves.append(value * sgn[h:h + 8])
            yield x, jnp.concatenate(halves, axis=0).astype(BF16)

    def gather(i, carry):
        start = pl.multiple_of(i * 16, 16)
        for x, value in take(source_ref[pl.ds(start, 16), :], sign_ref[pl.ds(start, 16), :]):
            dvec[pl.ds(start, 16), x * LANES:(x + 1) * LANES] = value
        return carry

    full = pairs // 16
    lax.fori_loop(0, full, gather, 0)
    rest = pairs - full * 16
    if rest:
        fill = jnp.zeros((16 - rest, LANES), jnp.int32)
        src = jnp.concatenate([source_ref[full * 16:pairs, :], fill], axis=0)
        sgn = jnp.concatenate([sign_ref[full * 16:pairs, :], fill], axis=0)
        for x, value in take(src, sgn):
            dvec[full * 16:full * 16 + 16, x * LANES:(x + 1) * LANES] = value

    partial = None
    for a in range(strings):
        evec = jnp.dot(ints_ref[...], dvec[0:pairs, 2 * a * LANES:2 * (a + 1) * LANES], preferred_element_type=F32)
        term = jnp.dot(counts[a], evec.astype(BF16), preferred_element_type=F32)
        partial = term if partial is None else partial + term
    for d in range(n_alpha):
        own = partial[d * strings:(d + 1) * strings]
        both = jnp.concatenate([own[:, :LANES], own[:, LANES:]], axis=0)
        blocks[d] = both
        sent[d] = both.astype(BF16)

    copies = []
    for r in range(1, n_alpha):
        to = lax.rem(ia + r, n_alpha)
        copy = pltpu.make_async_remote_copy(
            src_ref=sent.at[to], dst_ref=got.at[r], send_sem=b_send.at[r], recv_sem=b_recv.at[r],
            device_id={"alpha": to}, device_id_type=MESH)
        copy.start()
        copies.append(copy)
    total = blocks[ia]
    for r, copy in enumerate(copies, 1):
        copy.wait_recv()
        total = total + got[r].astype(F32)
    out_ref[:, 0, :] = total[:strings]
    out_ref[:, 1, :] = total[strings:]
    for copy in copies:
        copy.wait_send()


def local(n_alpha, n_beta, coeffs, integrals, beta_source, beta_sign, alpha_slots):
    strings, parts, cols = coeffs.shape
    pairs = integrals.shape[0]
    rows = strings * parts
    flat = coeffs.reshape(rows, cols)
    if cols < LANES:
        pad = ((0, 0), (0, LANES - cols))
        flat, beta_source, beta_sign = (jnp.pad(v, pad) for v in (flat, beta_source, beta_sign))
    vmem = pl.BlockSpec(memory_space=pltpu.VMEM)
    dma = pltpu.SemaphoreType.DMA
    out = pl.pallas_call(
        functools.partial(kernel, n_alpha, n_beta, cols, strings),
        out_shape=jax.ShapeDtypeStruct((strings, parts, LANES), F32),
        in_specs=[vmem] * 5,
        out_specs=vmem,
        scratch_shapes=[
            pltpu.VMEM((n_beta, rows, LANES), BF16),
            pltpu.VMEM((n_beta, rows, 8, LANES), F32),
            pltpu.VMEM((-(-pairs // 16) * 16, rows * LANES), BF16),
            pltpu.VMEM((strings, n_alpha * strings, pairs), BF16),
            pltpu.VMEM((n_alpha, rows, LANES), F32),
            pltpu.VMEM((n_alpha, rows, LANES), BF16),
            pltpu.VMEM((n_alpha, rows, LANES), BF16),
            dma((n_beta,)),
            dma((n_beta,)),
            dma((n_alpha,)),
            dma((n_alpha,)),
        ],
        compiler_params=pltpu.CompilerParams(
            collective_id=0, has_side_effects=True, vmem_limit_bytes=40 * 1024 * 1024),
    )(flat, integrals, beta_source, beta_sign, alpha_slots)
    return out[:, :, :cols]


def solution(mesh):
    in_specs = (
        P("alpha", None, "beta"),
        P(),
        P(None, "beta"),
        P(None, "beta"),
        P("alpha", None, None, None),
    )
    out_specs = P("alpha", None, "beta")
    fn = functools.partial(local, mesh.shape["alpha"], mesh.shape["beta"])
    return jax.shard_map(fn, mesh=mesh, in_specs=in_specs, out_specs=out_specs, check_vma=False)
```

time: 198 us -> 24.9 us (0.13)
  local copies, waits for them, and re-layouts: 149 us -> 4.97 us
  blocking collectives: 35.4 us -> 0 us
  Pallas kernels: 0 us -> 19.6 us
  starting transfers between devices: 8.31 us -> 0 us
  other arithmetic: 3.39 us -> 0 us
    gather x3 -> x0, local copies, waits for them, and re-layouts: 143 us -> none  [the longest x2 136 us: local(): taken = jnp.take(cols_mat, beta_source, axis=1)]
    all_to_all x1 -> x0, blocking collectives: 33.4 us -> none  [local(): lax.all_to_all(buffer, 'alpha', split_axis=0, concat_axis=0, tiled=True)]
    pallas_call x0 -> x1, Pallas kernels: none -> 19.6 us  [local(): pl.pallas_call(functools.partial(kernel, n_alpha, n_beta, cols, strings),...]
    all_to_all x1 -> x0, starting transfers between devices: 8.31 us -> none  [local(): lax.all_to_all(target_ids, 'alpha', split_axis=0, concat_axis=0, tiled=True)]
    unnamed x5 -> x11, local copies, waits for them, and re-layouts: 0.83 us -> 4.97 us
    reshape x4 -> x0, local copies, waits for them, and re-layouts: 3.37 us -> none  [the longest x1 2.62 us: local(): evec_sum.astype(jnp.bfloat16).reshape(pair_count * strings, 2 * beta_cols)]
    all_gather x1 -> x0, blocking collectives: 2.02 us -> none  [local(): all_cols = lax.all_gather(coeffs, 'beta', axis=2, tiled=True)]
  transfers between devices with their start and end apart: 1 -> 0, of which waited for: 0 -> 0; matrix products, arithmetic and copies ran while one was open for 77% -> 0% of each run, Pallas kernels for 0% -> 0%
where the time goes in v1:
time: 24.9 us; the launch traced here: 24.6 us
  Pallas kernels  19.6 us (79%)
  local copies, waits for them, and re-layouts  4.97 us (20%)
    pallas_call x1, Pallas kernels, local(): pl.pallas_call(functools.partial(kernel, n_alpha, n_beta, cols, strings),...  19.6 us
    unnamed x11, local copies, waits for them, and re-layouts  4.97 us

profile of v1, /device:TPU:0, one launch (start us, length us, event | category | flops | bytes accessed | tf_op | source)
XLA Modules:
  0.0 24.6 jit_solution(13104636356067930046)
XLA Ops:
  0.0 0.0 copy-start
  0.0 1.0 %copy-done = bf16[484,484]{1,0:T(8,128)(2,1)S(1)} copy-done((bf16[484,484]{1,0:T(8,128)(2,1)S(1)}, bf16[484,484]{1,0:T(8,128)(2,1)}, u32[]{:S(2)}) %copy-start) | copy-done | bytes 468536
  1.0 0.0 copy-start.1
  1.0 0.9 %copy-done.1 = s32[484,128]{1,0:T(8,128)S(1)} copy-done((s32[484,128]{1,0:T(8,128)S(1)}, s32[484,128]{1,0:T(8,128)}, u32[]{:S(2)}) %copy-start.1) | copy-done | bytes 247832
  2.0 0.0 copy-start.2
  2.0 0.9 %copy-done.2 = s32[484,128]{1,0:T(8,128)S(1)} copy-done((s32[484,128]{1,0:T(8,128)S(1)}, s32[484,128]{1,0:T(8,128)}, u32[]{:S(2)}) %copy-start.2) | copy-done | bytes 247832
  2.9 0.0 copy-start.3
  2.9 0.8 %copy-done.3 = s32[1,16,4,128]{3,2,1,0:T(4,128)S(1)} copy-done((s32[1,16,4,128]{3,2,1,0:T(4,128)S(1)}, s32[1,16,4,128]{3,2,1,0:T(4,128)}, u32[]{:S(2)}) %copy-start.3) | copy-done | bytes 32792
  3.7 0.0 copy-start.4
  3.7 0.7 %copy-done.4 = bf16[8,2,128]{2,1,0:T(2,128)(2,1)S(1)} copy-done((bf16[8,2,128]{2,1,0:T(2,128)(2,1)S(1)}, bf16[8,2,128]{2,1,0:T(2,128)(2,1)}, u32[]{:S(2)}) %copy-start.4) | copy-done | bytes 4120
  4.4 19.6 %shard_map.55 = f32[8,2,128]{2,1,0:T(2,128)S(1)} custom-call(bf16[16,128]{1,0:T(8,128)(2,1)S(1)} %bitcast.1, bf16[484,484]{1,0:T(8,128)(2,1)S(1)} %copy-done, s32[484,128]{1,0:T(8,128)S(1)} %copy-done.1, s32[484,128]{1,0:T(8,128)S(1)} %copy-done.2, s32[1,16,4,128]{3,2,1,0:T(4,128)S(1)} %copy-done.3), custom_call_target="tpu_custom_call" | custom-call | tf_op jit(solution)/shard_map/pallas_call | solution.py:141
  24.0 0.6 %copy.7 = f32[8,2,128]{2,1,0:T(2,128)} copy(f32[8,2,128]{2,1,0:T(2,128)S(1)} %shard_map.55) | data formatting | bytes 16384
Async XLA Ops:
  0.0 1.0 %copy-start = (bf16[484,484]{1,0:T(8,128)(2,1)S(1)}, bf16[484,484]{1,0:T(8,128)(2,1)}, u32[]{:S(2)}) copy-start(bf16[484,484]{1,0:T(8,128)(2,1)} %ints_ref.1) | copy-start | bytes 1405540
  1.0 0.9 %copy-start.1 = (s32[484,128]{1,0:T(8,128)S(1)}, s32[484,128]{1,0:T(8,128)}, u32[]{:S(2)}) copy-start(s32[484,128]{1,0:T(8,128)} %source_ref.1) | copy-start | bytes 743428
  2.0 0.9 %copy-start.2 = (s32[484,128]{1,0:T(8,128)S(1)}, s32[484,128]{1,0:T(8,128)}, u32[]{:S(2)}) copy-start(s32[484,128]{1,0:T(8,128)} %sign_ref.1) | copy-start | bytes 743428
  2.9 0.8 %copy-start.3 = (s32[1,16,4,128]{3,2,1,0:T(4,128)S(1)}, s32[1,16,4,128]{3,2,1,0:T(4,128)}, u32[]{:S(2)}) copy-start(s32[1,16,4,128]{3,2,1,0:T(4,128)} %slots_ref.1) | copy-start | bytes 98308
  3.7 0.7 %copy-start.4 = (bf16[8,2,128]{2,1,0:T(2,128)(2,1)S(1)}, bf16[8,2,128]{2,1,0:T(2,128)(2,1)}, u32[]{:S(2)}) copy-start(bf16[8,2,128]{2,1,0:T(2,128)(2,1)} %param.5) | copy-start | bytes 12292

commit v2 on v1

--- a/solution.py
+++ b/solution.py
@@ -15,14 +15,24 @@
 
 def kernel(
     n_alpha, n_beta, cols, strings,
-    coeffs_ref, ints_ref, source_ref, sign_ref, slots_ref, out_ref,
+    coeffs_hbm, ints_hbm, source_hbm, sign_hbm, slots_hbm, out_ref,
+    ints_ref, source_ref, sign_ref, slots_ref,
     table, wide, dvec, counts, blocks, sent, got,
-    c_send, c_recv, b_send, b_recv,
+    c_send, c_recv, b_send, b_recv, loaded,
 ):
     ia = lax.axis_index("alpha")
     ib = lax.axis_index("beta")
     pairs = ints_ref.shape[0]
     rows = 2 * strings
+
+    loads = [
+        pltpu.make_async_copy(src, dst, loaded.at[i])
+        for i, (src, dst) in enumerate((
+            (slots_hbm, slots_ref), (coeffs_hbm, table.at[0]), (source_hbm, source_ref),
+            (sign_hbm, sign_ref), (ints_hbm, ints_ref)))
+    ]
+    for load in loads:
+        load.start()
 
     barrier = pltpu.get_barrier_semaphore()
     for r in range(1, n_beta):
@@ -47,23 +57,26 @@
             counts[a, pl.ds(pl.multiple_of(j * rows, rows), rows), :] = both.astype(BF16)
         return carry
 
+    loads[0].wait()
     first = n_alpha // 4
-    lax.fori_loop(0, first, count, 0)
+    lax.fori_loop(0, first, count, 0, unroll=4)
     pl.semaphore_wait(barrier, n_alpha + n_beta - 2)
 
     copies = []
     for r in range(1, n_beta):
         copy = pltpu.make_async_remote_copy(
-            src_ref=coeffs_ref, dst_ref=table.at[r], send_sem=c_send.at[r], recv_sem=c_recv.at[r],
+            src_ref=coeffs_hbm, dst_ref=table.at[r], send_sem=c_send.at[r], recv_sem=c_recv.at[r],
             device_id={"beta": lax.rem(ib + r, n_beta)}, device_id_type=MESH)
         copy.start()
         copies.append(copy)
-    lax.fori_loop(first, n_alpha // 2, count, 0)
+    lax.fori_loop(first, n_alpha // 2, count, 0, unroll=4)
+    for load in loads[1:]:
+        load.wait()
     for copy in copies:
         copy.wait()
 
     for r in range(n_beta):
-        block = (coeffs_ref[...] if r == 0 else table[r]).astype(F32)
+        block = table[r].astype(F32)
         for x in range(rows):
             wide[r, x] = jnp.broadcast_to(block[x:x + 1], (8, LANES))
 
@@ -90,7 +103,7 @@
         return carry
 
     full = pairs // 16
-    lax.fori_loop(0, full, gather, 0)
+    lax.fori_loop(0, full, gather, 0, unroll=2)
     rest = pairs - full * 16
     if rest:
         fill = jnp.zeros((16 - rest, LANES), jnp.int32)
@@ -141,9 +154,13 @@
     out = pl.pallas_call(
         functools.partial(kernel, n_alpha, n_beta, cols, strings),
         out_shape=jax.ShapeDtypeStruct((strings, parts, LANES), F32),
-        in_specs=[vmem] * 5,
+        in_specs=[pl.BlockSpec(memory_space=pltpu.HBM)] * 5,
         out_specs=vmem,
         scratch_shapes=[
+            pltpu.VMEM(integrals.shape, BF16),
+            pltpu.VMEM(beta_source.shape, jnp.int32),
+            pltpu.VMEM(beta_sign.shape, jnp.int32),
+            pltpu.VMEM(alpha_slots.shape, jnp.int32),
             pltpu.VMEM((n_beta, rows, LANES), BF16),
             pltpu.VMEM((n_beta, rows, 8, LANES), F32),
             pltpu.VMEM((-(-pairs // 16) * 16, rows * LANES), BF16),
@@ -155,6 +172,7 @@
             dma((n_beta,)),
             dma((n_alpha,)),
             dma((n_alpha,)),
+            dma((5,)),
         ],
         compiler_params=pltpu.CompilerParams(
             collective_id=0, has_side_effects=True, vmem_limit_bytes=40 * 1024 * 1024),

time: 24.9 us -> 24.7 us (level)
  no operation moved by 1% of the time
where the time goes in v2:
time: 24.7 us; the launch traced here: 24.4 us
  Pallas kernels  19.4 us (79%)
  local copies, waits for them, and re-layouts  4.97 us (20%)
    pallas_call x1, Pallas kernels, local(): pl.pallas_call(functools.partial(kernel, n_alpha, n_beta, cols, strings),...  19.4 us
    unnamed x11, local copies, waits for them, and re-layouts  4.97 us

profile of v2, /device:TPU:0, one launch (start us, length us, event | category | flops | bytes accessed | tf_op | source)
XLA Modules:
  0.0 24.4 jit_solution(6972624313432133281)
XLA Ops:
  0.0 0.0 copy-start
  0.0 1.0 %copy-done = bf16[484,484]{1,0:T(8,128)(2,1)S(1)} copy-done((bf16[484,484]{1,0:T(8,128)(2,1)S(1)}, bf16[484,484]{1,0:T(8,128)(2,1)}, u32[]{:S(2)}) %copy-start) | copy-done | bytes 468536
  1.0 0.0 copy-start.1
  1.0 0.9 %copy-done.1 = s32[484,128]{1,0:T(8,128)S(1)} copy-done((s32[484,128]{1,0:T(8,128)S(1)}, s32[484,128]{1,0:T(8,128)}, u32[]{:S(2)}) %copy-start.1) | copy-done | bytes 247832
  2.0 0.0 copy-start.2
  2.0 0.9 %copy-done.2 = s32[484,128]{1,0:T(8,128)S(1)} copy-done((s32[484,128]{1,0:T(8,128)S(1)}, s32[484,128]{1,0:T(8,128)}, u32[]{:S(2)}) %copy-start.2) | copy-done | bytes 247832
  2.9 0.0 copy-start.3
  2.9 0.8 %copy-done.3 = s32[1,16,4,128]{3,2,1,0:T(4,128)S(1)} copy-done((s32[1,16,4,128]{3,2,1,0:T(4,128)S(1)}, s32[1,16,4,128]{3,2,1,0:T(4,128)}, u32[]{:S(2)}) %copy-start.3) | copy-done | bytes 32792
  3.7 0.0 copy-start.4
  3.7 0.7 %copy-done.4 = bf16[8,2,128]{2,1,0:T(2,128)(2,1)S(1)} copy-done((bf16[8,2,128]{2,1,0:T(2,128)(2,1)S(1)}, bf16[8,2,128]{2,1,0:T(2,128)(2,1)}, u32[]{:S(2)}) %copy-start.4) | copy-done | bytes 4120
  4.4 19.4 %shard_map.55 = f32[8,2,128]{2,1,0:T(2,128)S(1)} custom-call(bf16[16,128]{1,0:T(8,128)(2,1)S(1)} %bitcast.1, bf16[484,484]{1,0:T(8,128)(2,1)S(1)} %copy-done, s32[484,128]{1,0:T(8,128)S(1)} %copy-done.1, s32[484,128]{1,0:T(8,128)S(1)} %copy-done.2, s32[1,16,4,128]{3,2,1,0:T(4,128)S(1)} %copy-done.3), custom_call_target="tpu_custom_call" | custom-call | tf_op jit(solution)/shard_map/pallas_call | solution.py:154
  23.8 0.6 %copy.7 = f32[8,2,128]{2,1,0:T(2,128)} copy(f32[8,2,128]{2,1,0:T(2,128)S(1)} %shard_map.55) | data formatting | bytes 16384
Async XLA Ops:
  0.0 1.0 %copy-start = (bf16[484,484]{1,0:T(8,128)(2,1)S(1)}, bf16[484,484]{1,0:T(8,128)(2,1)}, u32[]{:S(2)}) copy-start(bf16[484,484]{1,0:T(8,128)(2,1)} %ints_hbm.1) | copy-start | bytes 1405540
  1.0 0.9 %copy-start.1 = (s32[484,128]{1,0:T(8,128)S(1)}, s32[484,128]{1,0:T(8,128)}, u32[]{:S(2)}) copy-start(s32[484,128]{1,0:T(8,128)} %source_hbm.1) | copy-start | bytes 743428
  2.0 0.9 %copy-start.2 = (s32[484,128]{1,0:T(8,128)S(1)}, s32[484,128]{1,0:T(8,128)}, u32[]{:S(2)}) copy-start(s32[484,128]{1,0:T(8,128)} %sign_hbm.1) | copy-start | bytes 743428
  2.9 0.8 %copy-start.3 = (s32[1,16,4,128]{3,2,1,0:T(4,128)S(1)}, s32[1,16,4,128]{3,2,1,0:T(4,128)}, u32[]{:S(2)}) copy-start(s32[1,16,4,128]{3,2,1,0:T(4,128)} %slots_hbm.1) | copy-start | bytes 98308
  3.7 0.7 %copy-start.4 = (bf16[8,2,128]{2,1,0:T(2,128)(2,1)S(1)}, bf16[8,2,128]{2,1,0:T(2,128)(2,1)}, u32[]{:S(2)}) copy-start(bf16[8,2,128]{2,1,0:T(2,128)(2,1)} %param.5) | copy-start | bytes 12292

commit v3 on v2

--- a/solution.py
+++ b/solution.py
@@ -175,7 +175,7 @@
             dma((5,)),
         ],
         compiler_params=pltpu.CompilerParams(
-            collective_id=0, has_side_effects=True, vmem_limit_bytes=40 * 1024 * 1024),
+            collective_id=0, has_side_effects=True, vmem_limit_bytes=63 * 1024 * 1024),
     )(flat, integrals, beta_source, beta_sign, alpha_slots)
     return out[:, :, :cols]
 

time: 24.7 us -> 20.9 us (0.85)
  local copies, waits for them, and re-layouts: 4.97 us -> 1.3 us
    unnamed x11 -> x1, local copies, waits for them, and re-layouts: 4.97 us -> 1.3 us
where the time goes in v3:
time: 20.9 us; the launch traced here: 20.7 us
  Pallas kernels  19.4 us (93%)
  local copies, waits for them, and re-layouts  1.3 us (6%)
    pallas_call x1, Pallas kernels, local(): pl.pallas_call(functools.partial(kernel, n_alpha, n_beta, cols, strings),...  19.4 us
    unnamed x1, local copies, waits for them, and re-layouts  1.3 us

profile of v3, /device:TPU:0, one launch (start us, length us, event | category | flops | bytes accessed | tf_op | source)
XLA Modules:
  0.0 20.7 jit_solution(15211412108147050927)
XLA Ops:
  0.0 19.4 %shard_map.55 = f32[8,2,128]{2,1,0:T(2,128)} custom-call(bf16[16,128]{1,0:T(8,128)(2,1)} %bitcast.1, bf16[484,484]{1,0:T(8,128)(2,1)} %ints_hbm.1, s32[484,128]{1,0:T(8,128)} %source_hbm.1, s32[484,128]{1,0:T(8,128)} %sign_hbm.1, s32[1,16,4,128]{3,2,1,0:T(4,128)} %slots_hbm.1), custom_call_target="tpu_custom_call" | custom-call | tf_op jit(solution)/shard_map/pallas_call | solution.py:154
  19.4 1.3 %copy.7 = f32[8,2,128]{2,1,0:T(2,128)} copy(f32[8,2,128]{2,1,0:T(2,128)} %shard_map.55) | data formatting | bytes 16384

commit v4 on v3

--- a/solution.py
+++ b/solution.py
@@ -80,12 +80,12 @@
         for x in range(rows):
             wide[r, x] = jnp.broadcast_to(block[x:x + 1], (8, LANES))
 
-    def take(src, sgn):
+    def take(src, sgn, span=range(rows)):
         lane = src & (cols - 1)
         step = lax.shift_right_logical(src, (cols - 1).bit_length())
         slot = (ib + n_beta - step) & (n_beta - 1)
         sgn = sgn.astype(F32)
-        for x in range(rows):
+        for x in span:
             halves = []
             for h in (0, 8):
                 index = lane[h:h + 8]
@@ -103,17 +103,29 @@
         return carry
 
     full = pairs // 16
-    lax.fori_loop(0, full, gather, 0, unroll=2)
     rest = pairs - full * 16
-    if rest:
-        fill = jnp.zeros((16 - rest, LANES), jnp.int32)
-        src = jnp.concatenate([source_ref[full * 16:pairs, :], fill], axis=0)
-        sgn = jnp.concatenate([sign_ref[full * 16:pairs, :], fill], axis=0)
-        for x, value in take(src, sgn):
-            dvec[full * 16:full * 16 + 16, x * LANES:(x + 1) * LANES] = value
+    inline = n_beta <= 2
+    if not inline:
+        lax.fori_loop(0, full, gather, 0, unroll=2)
+
+    def tile(i, span):
+        if i < full:
+            src, sgn = source_ref[i * 16:i * 16 + 16, :], sign_ref[i * 16:i * 16 + 16, :]
+        else:
+            fill = jnp.zeros((16 - rest, LANES), jnp.int32)
+            src = jnp.concatenate([source_ref[full * 16:pairs, :], fill], axis=0)
+            sgn = jnp.concatenate([sign_ref[full * 16:pairs, :], fill], axis=0)
+        for x, value in take(src, sgn, span):
+            dvec[i * 16:i * 16 + 16, x * LANES:(x + 1) * LANES] = value
+
+    if rest and not inline:
+        tile(full, range(rows))
 
     partial = None
     for a in range(strings):
+        if inline:
+            for i in range(-(-pairs // 16)):
+                tile(i, range(2 * a, 2 * a + 2))
         evec = jnp.dot(ints_ref[...], dvec[0:pairs, 2 * a * LANES:2 * (a + 1) * LANES], preferred_element_type=F32)
         term = jnp.dot(counts[a], evec.astype(BF16), preferred_element_type=F32)
         partial = term if partial is None else partial + term

time: 20.9 us -> 19.3 us (0.923)
  Pallas kernels: 19.4 us -> 17.8 us
    pallas_call x1, Pallas kernels: 19.4 us -> 17.8 us  [local(): pl.pallas_call(functools.partial(kernel, n_alpha, n_beta, cols, strings),...]
where the time goes in v4:
time: 19.3 us; the launch traced here: 19.1 us
  Pallas kernels  17.8 us (92%)
  local copies, waits for them, and re-layouts  1.3 us (7%)
    pallas_call x1, Pallas kernels, local(): pl.pallas_call(functools.partial(kernel, n_alpha, n_beta, cols, strings),...  17.8 us
    unnamed x1, local copies, waits for them, and re-layouts  1.3 us

profile of v4, /device:TPU:0, one launch (start us, length us, event | category | flops | bytes accessed | tf_op | source)
XLA Modules:
  0.0 19.1 jit_solution(10053140105332682159)
XLA Ops:
  0.0 17.8 %shard_map.55 = f32[8,2,128]{2,1,0:T(2,128)} custom-call(bf16[16,128]{1,0:T(8,128)(2,1)} %bitcast.1, bf16[484,484]{1,0:T(8,128)(2,1)} %ints_hbm.1, s32[484,128]{1,0:T(8,128)} %source_hbm.1, s32[484,128]{1,0:T(8,128)} %sign_hbm.1, s32[1,16,4,128]{3,2,1,0:T(4,128)} %slots_hbm.1), custom_call_target="tpu_custom_call" | custom-call | tf_op jit(solution)/shard_map/pallas_call | solution.py:166
  17.8 1.3 %copy.7 = f32[8,2,128]{2,1,0:T(2,128)} copy(f32[8,2,128]{2,1,0:T(2,128)} %shard_map.55) | data formatting | bytes 16384
